TPU v7x, 512 devices: a whole 4x4x16 slice. The times are simulated.
512 devices in a mesh: aa: 32 (over x, z_lo, core), ba: 16 (over y, z_hi).
Axes of the slice: x: 4, y: 4, z: 16 (z_hi: 4, z_lo: 4; z = z_hi * 4 + z_lo), core: 2. Of those that a mesh axis runs over, the one named last changes fastest.
Arguments:
- amplitudes: bfloat16 [1024, 2048], P('ba', 'aa'), may hold values from -6 to 6
- integrals: bfloat16 [512, 512, 2048], P('aa', 'ba'), may hold values from -0.125 to 0.125
- virt_energy: float32 [512], replicated, may hold values from 0.2 to 2
- pair_energy: float32 [1024], replicated, may hold values from 0.3 to 3
Outputs:
- update: float32 [512, 512, 1024], P('aa', 'ba')
All inputs are finite; a program needn't handle non-finite values.
Results may differ from a plain program's by a relative error of at most 0.0003.
Values may be sent and summed in bfloat16 or wider, within the bound.
No kernel may reach another device: no remote copies, remote signals or barrier semaphores. Data moves between devices by JAX's collectives and lax.ppermute only.
A program may use at most 64 MiB of HBM per device.

v0:
```python
import jax
import jax.numpy as jnp
from jax import lax
from jax.sharding import PartitionSpec as P


def contract(left, right):
    return lax.dot_general(
        left, right, (((1,), (1,)), ((), ())), preferred_element_type=jnp.float32
    )


def on_device(amplitudes, integrals, virt_energy, pair_energy):
    first_count = integrals.shape[0]
    second_count = integrals.shape[1]
    cd_count = integrals.shape[2]
    flat_ints = integrals.reshape(first_count * second_count, cd_count)
    all_rows = lax.all_gather(amplitudes, "ba", axis=0, tiled=True)
    whole = lax.all_gather(all_rows, "aa", axis=1, tiled=True)
    ladder = contract(flat_ints, whole)
    pair_total = ladder.shape[1]
    ladder = ladder.reshape(first_count, second_count, pair_total)
    first_energy = lax.dynamic_slice_in_dim(
        virt_energy, lax.axis_index("aa") * first_count, first_count, 0
    )
    second_energy = lax.dynamic_slice_in_dim(
        virt_energy, lax.axis_index("ba") * second_count, second_count, 0
    )
    denom = first_energy[:, None, None] + second_energy[None, :, None] + pair_energy[None, None, :]
    return ladder / denom


def solution(mesh):
    placed = (P("ba", "aa"), P("aa", "ba", None), P(), P())
    return jax.shard_map(
        on_device, mesh=mesh, in_specs=placed, out_specs=P("aa", "ba", None), check_vma=False
    )
```

profile of v0, /device:TPU:1, one launch (start us, length us, event | category | flops | bytes accessed | tf_op | source)
XLA Modules:
  0.0 142.0 jit_solution(13501410611730573716)
XLA Ops:
  6.5 0.0 copy-start
  6.5 0.0 all-gather.2.cloned.1.call-start
  6.5 54.3 %all_gather.6 = bf16[1024,64]{1,0:T(8,128)(2,1)S(1)} all-gather(bf16[64,64]{1,0:T(8,128)(2,1)} %param.4), channel_id=1, replica_groups=mesh['aa'=32,'ba'=16] {'ba'}, dimensions={0}, use_global_device_ids=true | all-gather | bytes 139264 | tf_op jit(solution)/shard_map/all_gather | solution.py:18
  60.8 0.8 copy.6
  61.6 0.0 all-gather.2.cloned.1.call-update
  61.6 0.8 dynamic_slice.7
  62.4 0.8 dynamic_slice.6
  63.1 0.1 broadcast_add_fusion
  63.2 66.1 %all-gather.2.cloned.1.call-done = bf16[1024,2048]{0,1:T(8,128)(2,1)} async-done(((bf16[1024,64]{0,1:T(8,128)(2,1)}), bf16[1024,2048]{0,1:T(8,128)(2,1)}) %all-gather.2.cloned.1.call-update) | async-done | bytes 4194320 | tf_op jit(solution)/shard_map/all_gather | solution.py:19
  129.3 0.0 copy-done
  129.3 5.8 %add_divide_fusion = f32[16,32,1024]{2,1,0:T(8,128)} fusion(bf16[16,32,2048]{2,1,0:T(8,128)(2,1)S(1)} %copy-done, bf16[1024,2048]{0,1:T(8,128)(2,1)} %all-gather.2.cloned.1.call-done, f32[1024]{0:T(1024)} %param.7, f32[16,32]{1,0:T(8,128)S(1)} %broadcast_add_fusion), kind=kOutput, calls=%fused_computation.2 | convolution fusion | flops 2148532224 | bytes 8394752 | tf_op jit(solution)/shard_map/dot_general | solution.py:8
Async XLA Ops:
  6.5 122.8 %copy-start = (bf16[16,32,2048]{2,1,0:T(8,128)(2,1)S(1)}, bf16[16,32,2048]{2,1,0:T(8,128)(2,1)}, u32[]{:S(2)}) copy-start(bf16[16,32,2048]{2,1,0:T(8,128)(2,1)} %param.5) | copy-start | bytes 6291460
  6.5 122.8 %all-gather.2.cloned.1.call-start = ((), (), s32[]{:S(2)}) async-start(), calls=%async_computation | async-start | bytes 4325376 | tf_op jit(solution)/shard_map/all_gather | solution.py:19
Sparse Core Ops, SparseCore 0:
  61.7 67.5 all-gather.1
where the time goes:
time: 142 us
  waiting for transfers between devices  66.1 us (47%)
  blocking collectives  54.3 us (38%)
  between operations  13.4 us (9%)
  matrix products  5.85 us (4%)
  local copies, waits for them, and re-layouts  2.3 us (2%)
    all_gather x1, waiting for transfers between devices, on_device(): whole = lax.all_gather(all_rows, 'aa', axis=1, tiled=True)  66.1 us
    all_gather x1, blocking collectives, on_device(): all_rows = lax.all_gather(amplitudes, 'ba', axis=0, tiled=True)  54.3 us
    dot_general x1, matrix products, contract(): lax.dot_general(left, right, (((1,), (1,)), ((), ())), preferred_element_...  5.85 us
  transfers between devices with their start and end apart: 1, of which 1 were waited for; matrix products, arithmetic and copies ran while one was open for 1% of the time, Pallas kernels for 0%

commit v1 on v0

v1 whole, which is shorter than its diff:
```python
import functools

import jax
import jax.numpy as jnp
from jax import lax
from jax.experimental import pallas as pl
from jax.experimental.pallas import tpu as pltpu
from jax.sharding import PartitionSpec as P

AXES = ("aa", "ba")
SIDE = 4
DEPTH = 16


def flat(x, y, z, core):
    z_hi, z_lo = divmod(z % DEPTH, SIDE)
    return (((x % SIDE) * SIDE + z_lo) * 2 + core) * DEPTH + (y % SIDE) * SIDE + z_hi


def z_groups():
    return [
        [flat(x, y, z, core) for z in range(DEPTH)]
        for x in range(SIDE) for y in range(SIDE) for core in range(2)
    ]


def plane_groups(x_core):
    return [
        [flat(i, u, z, core) if core == x_core else flat(u, i, z, core) for i in range(SIDE)]
        for u in range(SIDE) for z in range(DEPTH) for core in range(2)
    ]


def gather(block, groups):
    count = len(groups[0])
    sent = jnp.broadcast_to(block[None], (count, *block.shape))
    return lax.all_to_all(sent, AXES, 0, 0, axis_index_groups=groups, tiled=True)


def ladder_kernel(place_ref, ints_ref, own_ref, other_ref, energy_ref, pair_ref, out_ref, amps_ref):
    core = place_ref[0]
    lane = lax.broadcasted_iota(jnp.int32, (32, 128), 1)
    own_first = (lane < 64) == (core == 0)
    for y in range(SIDE):
        for x in range(SIDE):
            i = jnp.where(core == 0, y, x)
            j = jnp.where(core == 0, x, y)
            for z in range(DEPTH):
                own = own_ref[i, j, z]
                other = other_ref[j, i, z]
                z_hi, z_lo = divmod(z, SIDE)
                row = (y * SIDE + z_hi) * 64
                column = (x * SIDE + z_lo) * 128
                amps_ref[row : row + 32, column : column + 128] = jnp.where(own_first, own, other)
                swapped = jnp.where(own_first, other, own)
                amps_ref[row + 32 : row + 64, column : column + 128] = pltpu.roll(swapped, 64, 1)
    for n in range(0, 1024, 256):
        ladder = lax.dot_general(
            ints_ref[...], amps_ref[n : n + 256, :], (((1,), (1,)), ((), ())),
            preferred_element_type=jnp.float32,
        )
        out_ref[:, n : n + 256] = ladder / (energy_ref[...] + pair_ref[:, n : n + 256])


def on_device(amplitudes, integrals, virt_energy, pair_energy):
    first_count, second_count, cd_count = integrals.shape
    core = lax.rem(lax.axis_index("aa"), 2)
    upper, lower = amplitudes[:32], amplitudes[32:]
    left = jnp.where(core == 0, upper, lower)
    right = jnp.where(core == 0, lower, upper)
    block = jnp.concatenate([left, right], axis=1)
    block = gather(block, z_groups()).reshape(1, DEPTH * 32, 128)[0]
    block = gather(block, plane_groups(0)).reshape(SIDE * DEPTH * 32, 128)
    own = gather(block, plane_groups(1)).reshape(SIDE, SIDE, DEPTH, 32, 128)
    across = [(i, i ^ 1) for i in range(lax.axis_size("aa"))]
    other = lax.ppermute(own, "aa", across)

    first_energy = lax.dynamic_slice_in_dim(
        virt_energy, lax.axis_index("aa") * first_count, first_count, 0
    )
    second_energy = lax.dynamic_slice_in_dim(
        virt_energy, lax.axis_index("ba") * second_count, second_count, 0
    )
    energy = (first_energy[:, None] + second_energy[None, :]).reshape(-1, 1)
    rows, pairs = first_count * second_count, pair_energy.shape[0]
    vmem = pl.BlockSpec(memory_space=pltpu.VMEM)
    update = pl.pallas_call(
        ladder_kernel,
        out_shape=jax.ShapeDtypeStruct((rows, pairs), jnp.float32),
        in_specs=[pl.BlockSpec(memory_space=pltpu.SMEM)] + [vmem] * 5,
        out_specs=vmem,
        scratch_shapes=[pltpu.VMEM((pairs, cd_count), jnp.bfloat16)],
        compiler_params=pltpu.CompilerParams(vmem_limit_bytes=40 * 2**20),
        cost_estimate=pl.CostEstimate(flops=2 * rows * pairs * cd_count, bytes_accessed=2**23, transcendentals=0),
    )(
        core.reshape(1).astype(jnp.int32), integrals.reshape(rows, cd_count), own, other,
        energy, pair_energy.reshape(1, -1),
    )
    return update.reshape(first_count, second_count, pairs)


def solution(mesh):
    placed = (P("ba", "aa"), P("aa", "ba", None), P(), P())
    return jax.shard_map(
        on_device, mesh=mesh, in_specs=placed, out_specs=P("aa", "ba", None), check_vma=False
    )
```

time: 142 us -> 78.8 us (0.55)
  waiting for transfers between devices: 66.1 us -> 3.39 us
  between operations: 13.4 us -> 0.06 us
  starting transfers between devices: 0.01 us -> 8.12 us
  matrix products: 5.85 us -> 0 us
  Pallas kernels: 0 us -> 5.71 us
  blocking collectives: 54.3 us -> 57.9 us
    all_gather x1 -> x0, waiting for transfers between devices: 66.1 us -> none  [on_device(): whole = lax.all_gather(all_rows, 'aa', axis=1, tiled=True)]
    all_to_all x0 -> x3, blocking collectives: none -> 57.9 us  [gather(): lax.all_to_all(sent, AXES, 0, 0, axis_index_groups=groups, tiled=True)]
    all_gather x1 -> x0, blocking collectives: 54.3 us -> none  [on_device(): all_rows = lax.all_gather(amplitudes, 'ba', axis=0, tiled=True)]
    ppermute x0 -> x1, starting transfers between devices: none -> 8.12 us  [on_device(): other = lax.ppermute(own, 'aa', across)]
    dot_general x1 -> x0, matrix products: 5.85 us -> none  [contract(): lax.dot_general(left, right, (((1,), (1,)), ((), ())), preferred_element_...]
    pallas_call x0 -> x1, Pallas kernels: none -> 5.71 us  [on_device(): pl.pallas_call(ladder_kernel, out_shape=jax.ShapeDtypeStruct((rows, pairs...]
    ppermute x0 -> x1, waiting for transfers between devices: none -> 3.39 us  [on_device(): other = lax.ppermute(own, 'aa', across)]
    unnamed x2 -> x6, local copies, waits for them, and re-layouts: 0.01 us -> 1.6 us
where the time goes in v1:
time: 78.8 us; the launch traced here: 78.5 us
  blocking collectives  57.9 us (73%)
  starting transfers between devices  8.12 us (10%)
  Pallas kernels  5.71 us (7%)
  waiting for transfers between devices  3.39 us (4%)
  local copies, waits for them, and re-layouts  2.37 us (3%)
  other arithmetic  0.87 us (1%)
    all_to_all x3, blocking collectives, gather(): lax.all_to_all(sent, AXES, 0, 0, axis_index_groups=groups, tiled=True)  57.9 us
    ppermute x1, starting transfers between devices, on_device(): other = lax.ppermute(own, 'aa', across)  8.12 us
    pallas_call x1, Pallas kernels, on_device(): pl.pallas_call(ladder_kernel, out_shape=jax.ShapeDtypeStruct((rows, pairs...  5.71 us
    ppermute x1, waiting for transfers between devices, on_device(): other = lax.ppermute(own, 'aa', across)  3.39 us
    unnamed x6, local copies, waits for them, and re-layouts  1.6 us
  transfers between devices with their start and end apart: 1, of which 1 were waited for; matrix products, arithmetic and copies ran while one was open for 1% of the time, Pallas kernels for 0%

profile of v1, /device:TPU:1, one launch (start us, length us, event | category | flops | bytes accessed | tf_op | source)
XLA Modules:
  0.0 78.5 jit_solution(2191694723883218787)
XLA Ops:
  0.0 0.7 broadcast_select_fusion.1
  0.7 0.1 pad_maximum_fusion
  0.8 27.5 %all_to_all.15 = bf16[16,32,128]{2,1,0:T(8,128)(2,1)S(1)} all-to-all(bf16[16,32,128]{2,1,0:T(8,128)(2,1)S(1)} %broadcast_in_dim.10), channel_id=1, replica_groups={{0,32,64,96,1,33,65,97,2,34,66,98,3,35,67,99},{16,48,80,112,17,49,81,11..., dimensions={0} | all-to-all | bytes 262144 | tf_op jit(solution)/shard_map/all_to_all | solution.py:37
  28.4 0.1 broadcast_in_dim.24
  28.4 10.9 %all_to_all.16 = bf16[4,512,128]{2,1,0:T(8,128)(2,1)S(1)} all-to-all(bf16[4,512,128]{2,1,0:T(8,128)(2,1)S(1)} %broadcast_in_dim.24), channel_id=1, replica_groups={{0,128,256,384},{16,20,24,28},{32,160,288,416},{48,52,56,60},{64,192,32..., dimensions={0} | all-to-all | bytes 1048576 | tf_op jit(solution)/shard_map/all_to_all | solution.py:37
  39.4 0.3 broadcast_in_dim.26
  39.6 0.0 copy-start.2
  39.6 0.0 copy-start.1
  39.7 19.5 %all_to_all.17 = bf16[4,2048,128]{2,1,0:T(8,128)(2,1)S(1)} all-to-all(bf16[4,2048,128]{2,1,0:T(8,128)(2,1)S(1)} %broadcast_in_dim.26), channel_id=1, replica_groups={{0,4,8,12},{16,144,272,400},{32,36,40,44},{48,176,304,432},{64,68,72,76..., dimensions={0} | all-to-all | bytes 4194304 | tf_op jit(solution)/shard_map/all_to_all | solution.py:37
  59.1 8.1 %collective-permute-start = (bf16[4,4,16,32,128]{4,3,2,1,0:T(8,128)(2,1)S(1)}, bf16[4,4,16,32,128]{4,3,2,1,0:T(8,128)(2,1)}, u32[]{:S(2)}, u32[]{:S(2)}) collective-permute-start(bf16[4,4,16,32,128]{4,3,2,1,0:T(8,128)(2,1)S(1)} %bitcast.7), channel_id=1, source_target_pairs={{0,16},{16,0},{32,48},{48,32},{64,80},{80,64},{96,112},{112,96},{1... | collective-permute-start | bytes 6291464 | tf_op jit(solution)/shard_map/ppermute | solution.py:76
  67.3 0.0 copy-done.2
  67.3 0.1 dynamic_slice.7
  67.3 0.1 dynamic_slice.6
  67.4 0.1 broadcast_add_fusion
  67.5 0.3 add.35.energy_ref
  67.8 3.4 %collective-permute-done.other_ref = bf16[4,4,16,32,128]{4,3,2,1,0:T(8,128)(2,1)} collective-permute-done((bf16[4,4,16,32,128]{4,3,2,1,0:T(8,128)(2,1)S(1)}, bf16[4,4,16,32,128]{4,3,2,1,0:T(8,128)(2,1)}, u32[]{:S(2)}, u32[]{:S(2)}) %collective-permute-start) | collective-permute-done | bytes 2097184 | tf_op jit(solution)/shard_map/ppermute | solution.py:76
  71.1 0.0 copy-done.1
  71.2 0.0 copy-start
  71.2 1.6 %copy-done = bf16[16,32,2048]{2,1,0:T(8,128)(2,1)S(1)} copy-done((bf16[16,32,2048]{2,1,0:T(8,128)(2,1)S(1)}, bf16[16,32,2048]{2,1,0:T(8,128)(2,1)}, u32[]{:S(2)}) %copy-start) | copy-done | bytes 2097176
  72.7 5.7 %shard_map.46 = f32[512,1024]{1,0:T(8,128)} custom-call(s32[1]{0:T(128)} %bitcast.place_ref, bf16[512,2048]{1,0:T(8,128)(2,1)S(1)} %bitcast.9, bf16[4,4,16,32,128]{4,3,2,1,0:T(8,128)(2,1)S(1)} %bitcast.8, bf16[4,4,16,32,128]{4,3,2,1,0:T(8,128)(2,1)} %collective-permute-done.other_ref, f32[512,1]{1,0:T(8,128)S(1)} %add.35.energy_ref, f32[1,1024]{1,0:T(1,128)S(1)} %bitcast.10), custom_call_target="tpu_custom_call" | custom-call | flops 2147483648 | bytes 8388608 | tf_op jit(solution)/shard_map/pallas_call | solution.py:87
  (1 shorter events, 0.0 us)
Async XLA Ops:
  39.6 27.6 %copy-start.2 = (f32[512]{0:T(512)S(1)}, f32[512]{0:T(512)}, u32[]{:S(2)}) copy-start(f32[512]{0:T(512)} %param.6) | copy-start | bytes 6148
  39.6 31.5 %copy-start.1 = (f32[1024]{0:T(1024)S(1)}, f32[1024]{0:T(1024)}, u32[]{:S(2)}) copy-start(f32[1024]{0:T(1024)} %param.7) | copy-start | bytes 12292
  59.1 12.0 %collective-permute-start = (bf16[4,4,16,32,128]{4,3,2,1,0:T(8,128)(2,1)S(1)}, bf16[4,4,16,32,128]{4,3,2,1,0:T(8,128)(2,1)}, u32[]{:S(2)}, u32[]{:S(2)}) collective-permute-start(bf16[4,4,16,32,128]{4,3,2,1,0:T(8,128)(2,1)S(1)} %bitcast.7), channel_id=1, source_target_pairs={{0,16},{16,0},{32,48},{48,32},{64,80},{80,64},{96,112},{112,96},{1... | collective-permute-start | bytes 6291464 | tf_op jit(solution)/shard_map/ppermute | solution.py:76
  71.2 1.6 %copy-start = (bf16[16,32,2048]{2,1,0:T(8,128)(2,1)S(1)}, bf16[16,32,2048]{2,1,0:T(8,128)(2,1)}, u32[]{:S(2)}) copy-start(bf16[16,32,2048]{2,1,0:T(8,128)(2,1)} %param.5) | copy-start | bytes 6291460

commit v2 on v0

v2 whole, which is shorter than its diff:
```python
import functools

import jax
import jax.numpy as jnp
from jax import lax
from jax.experimental import pallas as pl
from jax.experimental.pallas import tpu as pltpu
from jax.sharding import PartitionSpec as P

AXES = ("aa", "ba")
SIDE = 4
DEPTH = 16
FIRSTS, SECONDS = 16, 32
TILE = 256


def flat(x, y, z, core):
    z_hi, z_lo = divmod(z % DEPTH, SIDE)
    return (((x % SIDE) * SIDE + z_lo) * 2 + core) * DEPTH + (y % SIDE) * SIDE + z_hi


def everywhere():
    return [
        (x, y, z, core)
        for x in range(SIDE) for y in range(SIDE) for z in range(DEPTH) for core in range(2)
    ]


def z_groups():
    return [
        [flat(x, y, z, core) for z in range(DEPTH)]
        for x in range(SIDE) for y in range(SIDE) for core in range(2)
    ]


def first_groups():
    return [
        [flat(i, u, z, core) if core == 0 else flat(u, i, z, core) for i in range(SIDE)]
        for u in range(SIDE) for z in range(DEPTH) for core in range(2)
    ]


def second_step(step):
    return [
        (flat(x, y, z, core), flat(x, y + step, z, core) if core == 0 else flat(x + step, y, z, core))
        for x, y, z, core in everywhere()
    ]


def core_swap():
    return [(flat(x, y, z, core), flat(x, y, z, 1 - core)) for x, y, z, core in everywhere()]


def where_am_i():
    aa, ba = lax.axis_index("aa"), lax.axis_index("ba")
    return lax.rem(aa, 2), lax.div(aa, 2 * SIDE), lax.div(ba, SIDE)


def line_kernel(in_ref, out_ref):
    low = lax.broadcasted_iota(jnp.int32, (32, 128), 1) < 64
    for z_hi in range(SIDE):
        for half in range(2):
            first = in_ref[z_hi * SIDE + 2 * half]
            second = in_ref[z_hi * SIDE + 2 * half + 1]
            upper = jnp.where(low, first, pltpu.roll(second, 64, 1))
            lower = jnp.where(low, pltpu.roll(first, 64, 1), second)
            row, column = z_hi * 64, half * 128
            for copy in range(SIDE):
                out_ref[copy, row : row + 32, column : column + 128] = upper
                out_ref[copy, row + 32 : row + 64, column : column + 128] = lower


def add_tiles(total_ref, ints_ref, mine_ref, other_ref, behind):
    core, x, y = where_am_i()
    x_from = lax.rem(x + SIDE - behind, SIDE)
    y_from = lax.rem(y + SIDE - behind, SIDE)

    def add(at_y, at_x, at_core, block):
        total_ref[at_y] += lax.dot_general(
            ints_ref[at_core, at_x], block, (((1,), (1,)), ((), ())),
            preferred_element_type=jnp.float32,
        )

    zero = core == 0
    for i in range(SIDE):
        add(jnp.where(zero, y_from, i), jnp.where(zero, i, x_from), core, mine_ref[i])
        add(jnp.where(zero, i, y_from), jnp.where(zero, x_from, i), 1 - core, other_ref[i])


def begin_kernel(virt_ref, raw_ref, pair_ref, later_ref, ints_ref, scale_ref):
    low = lax.broadcasted_iota(jnp.int32, (raw_ref.shape[0], 128), 1) < 64
    for x in range(SIDE):
        for half in range(2):
            column = x * 512 + half * 256
            first = raw_ref[:, column : column + 128]
            second = raw_ref[:, column + 128 : column + 256]
            to = slice(half * 128, half * 128 + 128)
            ints_ref[0, x, :, to] = jnp.where(low, first, pltpu.roll(second, 64, 1))
            ints_ref[1, x, :, to] = jnp.where(low, pltpu.roll(first, 64, 1), second)
    first_at, second_at = lax.axis_index("aa") * FIRSTS, lax.axis_index("ba") * SECONDS
    row = lax.broadcasted_iota(jnp.int32, (SECONDS, TILE), 0)
    seconds = jnp.zeros((SECONDS, TILE), jnp.float32)
    for b in range(SECONDS):
        seconds = jnp.where(row == b, virt_ref[second_at + b], seconds)
    for y in range(SIDE):
        pair = pair_ref[:, y * TILE : (y + 1) * TILE]
        for a in range(FIRSTS):
            denominator = virt_ref[first_at + a] + seconds + pair
            scale_ref[y, a * SECONDS : (a + 1) * SECONDS] = 1.0 / denominator


def plain_kernel(in_ref, out_ref):
    out_ref[...] = in_ref[...]


def copy_kernel(in_ref, later_ref, out_ref):
    out_ref[...] = in_ref[...]


def stack_kernel(*refs):
    for i, ref in enumerate(refs[:-1]):
        refs[-1][i] = ref[...]


def middle_kernel(ints_ref, near_ref, others_ref, total_ref):
    total_ref[...] = jnp.zeros(total_ref.shape, jnp.float32)
    for i, behind in enumerate((0, 1, 3)):
        add_tiles(total_ref, ints_ref, near_ref.at[i], others_ref.at[i], behind)


def end_kernel(ints_ref, mine_ref, other_ref, scale_ref, start_ref, out_ref, total_ref):
    for y in range(SIDE):
        total_ref[y] = start_ref[y]
    add_tiles(total_ref, ints_ref, mine_ref, other_ref, 2)
    for y in range(SIDE):
        out_ref[:, y * TILE : (y + 1) * TILE] = total_ref[y] * scale_ref[y]


SMEM = pl.BlockSpec(memory_space=pltpu.SMEM)
VMEM = pl.BlockSpec(memory_space=pltpu.VMEM)
LATER = pl.BlockSpec(memory_space=pl.ANY)


def call(kernel, ins, outs, specs=None, scratch=(), tiles=0, megabytes=16):
    return pl.pallas_call(
        kernel,
        out_shape=outs,
        in_specs=specs or [VMEM] * len(ins),
        out_specs=jax.tree.map(lambda _: VMEM, outs),
        scratch_shapes=list(scratch),
        compiler_params=pltpu.CompilerParams(vmem_limit_bytes=megabytes * 2**20),
        cost_estimate=pl.CostEstimate(
            flops=tiles * 2 * 512 * TILE * TILE, bytes_accessed=2**18, transcendentals=0
        ),
    )(*ins)


def bf16(*shape):
    return jax.ShapeDtypeStruct(shape, jnp.bfloat16)


def on_device(amplitudes, integrals, virt_energy, pair_energy):
    first_count, second_count, cd_count = integrals.shape
    rows, pairs = first_count * second_count, pair_energy.shape[0]

    packed = jnp.concatenate([amplitudes[:32], amplitudes[32:]], axis=1)
    sent = jnp.broadcast_to(packed[None], (DEPTH, 32, 128))
    lines = lax.all_to_all(sent, AXES, 0, 0, axis_index_groups=z_groups(), tiled=True)
    sent = call(line_kernel, (lines,), bf16(SIDE, TILE, TILE), megabytes=4)
    mine = lax.all_to_all(sent, AXES, 0, 0, axis_index_groups=first_groups(), tiled=True)

    before = lax.ppermute(mine, AXES, second_step(1))
    after = lax.ppermute(mine, AXES, second_step(-1))
    totals = jax.ShapeDtypeStruct((SIDE, rows, TILE), jnp.float32)
    ints, scale = call(
        begin_kernel,
        (virt_energy, integrals.reshape(rows, cd_count), pair_energy.reshape(1, -1), mine),
        (bf16(2, SIDE, rows, TILE), totals),
        specs=[SMEM, VMEM, VMEM, LATER], tiles=4,
    )
    relayed = call(copy_kernel, (before, scale), bf16(SIDE, TILE, TILE), specs=[VMEM, LATER], megabytes=2)
    far = lax.ppermute(relayed, AXES, second_step(1))
    near = call(stack_kernel, (mine, before, after), bf16(3, SIDE, TILE, TILE), megabytes=4)
    others = lax.ppermute(near, AXES, core_swap())
    far = call(plain_kernel, (far,), bf16(SIDE, TILE, TILE), tiles=400, megabytes=2)
    other_far = lax.ppermute(far, AXES, core_swap())
    total = call(middle_kernel, (ints, near, others), totals, tiles=24)
    update = call(
        end_kernel,
        (ints, far, other_far, scale, total),
        jax.ShapeDtypeStruct((rows, pairs), jnp.float32),
        scratch=[pltpu.VMEM((SIDE, rows, TILE), jnp.float32)],
        tiles=8,
    )
    return update.reshape(first_count, second_count, pairs)


def solution(mesh):
    placed = (P("ba", "aa"), P("aa", "ba", None), P(), P())
    return jax.shard_map(
        on_device, mesh=mesh, in_specs=placed, out_specs=P("aa", "ba", None), check_vma=False
    )
```

time: 142 us -> 79 us (0.56)
  waiting for transfers between devices: 66.1 us -> 4.45 us
  starting transfers between devices: 0.01 us -> 25.3 us
  blocking collectives: 54.3 us -> 38.5 us
  between operations: 13.4 us -> 0.14 us
  Pallas kernels: 0 us -> 9.36 us
  matrix products: 5.85 us -> 0 us
    all_gather x1 -> x0, waiting for transfers between devices: 66.1 us -> none  [on_device(): whole = lax.all_gather(all_rows, 'aa', axis=1, tiled=True)]
    all_gather x1 -> x0, blocking collectives: 54.3 us -> none  [on_device(): all_rows = lax.all_gather(amplitudes, 'ba', axis=0, tiled=True)]
    all_to_all x0 -> x2, blocking collectives: none -> 38.5 us  [the longest x1 27.5 us: on_device(): lax.all_to_all(sent, AXES, 0, 0, axis_index_groups=z_groups(), tiled=True)]
    ppermute x0 -> x5, starting transfers between devices: none -> 25.3 us  [the longest x1 8.83 us: on_device(): other_far = lax.ppermute(far, AXES, core_swap())]
    pallas_call x0 -> x7, Pallas kernels: none -> 9.36 us  [call(): pl.pallas_call(kernel, out_shape=outs, in_specs=specs or [VMEM] * len(ins...]
    dot_general x1 -> x0, matrix products: 5.85 us -> none  [contract(): lax.dot_general(left, right, (((1,), (1,)), ((), ())), preferred_element_...]
    ppermute x0 -> x5, waiting for transfers between devices: none -> 4.45 us  [the longest x1 3.4 us: on_device(): before = lax.ppermute(mine, AXES, second_step(1))]
    dynamic_slice x2 -> x0, local copies, waits for them, and re-layouts: 1.51 us -> none  [the longest x1 0.76 us: on_device(): lax.dynamic_slice_in_dim(virt_energy, lax.axis_index('ba') * second_count...]
  transfers between devices with their start and end apart: 1 -> 5, of which waited for: 1 -> 2; matrix products, arithmetic and copies ran while one was open for 1% -> 0% of each run, Pallas kernels for 0% -> 8%
where the time goes in v2:
time: 79 us; the launch traced here: 78.7 us
  blocking collectives  38.5 us (49%)
  starting transfers between devices  25.3 us (32%)
  Pallas kernels  9.36 us (12%)
  waiting for transfers between devices  4.45 us (6%)
  local copies, waits for them, and re-layouts  0.9 us (1%)
    all_to_all x1, blocking collectives, on_device(): lax.all_to_all(sent, AXES, 0, 0, axis_index_groups=z_groups(), tiled=True)  27.5 us
    all_to_all x1, blocking collectives, on_device(): lax.all_to_all(sent, AXES, 0, 0, axis_index_groups=first_groups(), tiled=...  10.9 us
    pallas_call x7, Pallas kernels, call(): pl.pallas_call(kernel, out_shape=outs, in_specs=specs or [VMEM] * len(ins...  9.36 us
    ppermute x1, starting transfers between devices, on_device(): other_far = lax.ppermute(far, AXES, core_swap())  8.83 us
    ppermute x1, starting transfers between devices, on_device(): others = lax.ppermute(near, AXES, core_swap())  8.03 us
    ppermute x1, waiting for transfers between devices, on_device(): before = lax.ppermute(mine, AXES, second_step(1))  3.4 us
    ppermute x1, starting transfers between devices, on_device(): after = lax.ppermute(mine, AXES, second_step(-1))  3.37 us
    ppermute x1, starting transfers between devices, on_device(): before = lax.ppermute(mine, AXES, second_step(1))  3.11 us
  transfers between devices with their start and end apart: 5, of which 2 were waited for; matrix products, arithmetic and copies ran while one was open for 0% of the time, Pallas kernels for 8%

profile of v2, /device:TPU:1, one launch (start us, length us, event | category | flops | bytes accessed | tf_op | source)
XLA Modules:
  0.0 78.7 jit_solution(1266301275849204146)
XLA Ops:
  0.0 0.0 copy-start.1
  0.0 0.0 copy-start.2
  0.0 0.0 copy-start
  0.0 0.9 %fusion = (bf16[32,64]{1,0:T(8,128)(2,1)S(1)}, bf16[32,64]{1,0:T(8,128)(2,1)S(1)}) fusion(bf16[64,64]{1,0:T(8,128)(2,1)} %param.4), kind=kLoop, calls=%fused_computation.1 | loop fusion | bytes 16384 | tf_op jit(solution)/shard_map/slice | solution.py:166
  0.9 0.1 pad_maximum_fusion
  1.0 27.5 %all_to_all.10.in_ref = bf16[16,32,128]{2,1,0:T(8,128)(2,1)S(1)} all-to-all(bf16[16,32,128]{2,1,0:T(8,128)(2,1)S(1)} %broadcast_in_dim.2), channel_id=1, replica_groups={{0,32,64,96,1,33,65,97,2,34,66,98,3,35,67,99},{16,48,80,112,17,49,81,11..., dimensions={0} | all-to-all | bytes 262144 | tf_op jit(solution)/shard_map/all_to_all | solution.py:168
  28.5 0.1 shard_map.46
  28.7 10.9 %all_to_all.11.later_ref.refs_0_ = bf16[4,256,256]{2,1,0:T(8,128)(2,1)S(1)} all-to-all(bf16[4,256,256]{2,1,0:T(8,128)(2,1)S(1)} %shard_map.46), channel_id=1, replica_groups={{0,128,256,384},{16,20,24,28},{32,160,288,416},{48,52,56,60},{64,192,32..., dimensions={0} | all-to-all | bytes 1048576 | tf_op jit(solution)/shard_map/all_to_all | solution.py:170
  39.6 3.1 %collective-permute-start = (bf16[4,256,256]{2,1,0:T(8,128)(2,1)S(1)}, bf16[4,256,256]{2,1,0:T(8,128)(2,1)S(1)}, u32[]{:S(2)}, u32[]{:S(2)}) collective-permute-start(bf16[4,256,256]{2,1,0:T(8,128)(2,1)S(1)} %all_to_all.11.later_ref.refs_0_), channel_id=1, source_target_pairs={{0,4},{16,144},{32,36},{48,176},{64,68},{80,208},{96,100},{112,240... | collective-permute-start | bytes 1572872 | tf_op jit(solution)/shard_map/ppermute | solution.py:172
  42.7 3.4 %collective-permute-start.3 = (bf16[4,256,256]{2,1,0:T(8,128)(2,1)S(1)}, bf16[4,256,256]{2,1,0:T(8,128)(2,1)S(1)}, u32[]{:S(2)}, u32[]{:S(2)}) collective-permute-start(bf16[4,256,256]{2,1,0:T(8,128)(2,1)S(1)} %all_to_all.11.later_ref.refs_0_), channel_id=1, source_target_pairs={{0,12},{16,400},{32,44},{48,432},{64,76},{80,464},{96,108},{112,49... | collective-permute-start | bytes 1572872 | tf_op jit(solution)/shard_map/ppermute | solution.py:173
  46.1 0.0 copy-done.1
  46.1 0.0 copy-done.2
  46.1 0.0 copy-done
  46.1 1.5 %shard_map.47 = (bf16[2,4,512,256]{3,2,1,0:T(8,128)(2,1)S(1)}, f32[4,512,256]{2,1,0:T(8,128)S(1)}) custom-call(f32[512]{0:T(512)S(1)} %copy-done.2, bf16[512,2048]{1,0:T(8,128)(2,1)S(1)} %bitcast.3, f32[1,1024]{1,0:T(1,128)S(1)} %bitcast.4, bf16[4,256,256]{2,1,0:T(8,128)(2,1)S(1)} %all_to_all.11.later_ref.refs_0_), custom_call_target="tpu_custom_call" | custom-call | flops 268435456 | bytes 262144 | tf_op jit(solution)/shard_map/pallas_call | solution.py:145
  47.6 3.4 %collective-permute-done.in_ref.refs_1_ = bf16[4,256,256]{2,1,0:T(8,128)(2,1)S(1)} collective-permute-done((bf16[4,256,256]{2,1,0:T(8,128)(2,1)S(1)}, bf16[4,256,256]{2,1,0:T(8,128)(2,1)S(1)}, u32[]{:S(2)}, u32[]{:S(2)}) %collective-permute-start) | collective-permute-done | bytes 524320 | tf_op jit(solution)/shard_map/ppermute | solution.py:172
  51.0 1.9 %collective-permute-start.1 = (bf16[4,256,256]{2,1,0:T(8,128)(2,1)S(1)}, bf16[4,256,256]{2,1,0:T(8,128)(2,1)S(1)}, u32[]{:S(2)}, u32[]{:S(2)}) collective-permute-start(bf16[4,256,256]{2,1,0:T(8,128)(2,1)S(1)} %shard_map.48), channel_id=1, source_target_pairs={{0,4},{16,144},{32,36},{48,176},{64,68},{80,208},{96,100},{112,240... | collective-permute-start | bytes 1572872 | tf_op jit(solution)/shard_map/ppermute | solution.py:182
  53.0 0.0 collective-permute-done.3.refs_2_
  53.0 0.1 shard_map.50.near_ref
  53.1 8.0 %collective-permute-start.4 = (bf16[3,4,256,256]{3,2,1,0:T(8,128)(2,1)S(1)}, bf16[3,4,256,256]{3,2,1,0:T(8,128)(2,1)S(1)}, u32[]{:S(2)}, u32[]{:S(2)}) collective-permute-start(bf16[3,4,256,256]{3,2,1,0:T(8,128)(2,1)S(1)} %shard_map.50.near_ref), channel_id=1, source_target_pairs={{0,16},{16,0},{32,48},{48,32},{64,80},{80,64},{96,112},{112,96},{1... | collective-permute-start | bytes 4718600 | tf_op jit(solution)/shard_map/ppermute | solution.py:184
  61.1 1.0 %collective-permute-done.1.in_ref = bf16[4,256,256]{2,1,0:T(8,128)(2,1)S(1)} collective-permute-done((bf16[4,256,256]{2,1,0:T(8,128)(2,1)S(1)}, bf16[4,256,256]{2,1,0:T(8,128)(2,1)S(1)}, u32[]{:S(2)}, u32[]{:S(2)}) %collective-permute-start.1) | collective-permute-done | bytes 524320 | tf_op jit(solution)/shard_map/ppermute | solution.py:182
  62.2 8.8 %collective-permute-start.2 = (bf16[4,256,256]{2,1,0:T(8,128)(2,1)S(1)}, bf16[4,256,256]{2,1,0:T(8,128)(2,1)S(1)}, u32[]{:S(2)}, u32[]{:S(2)}) collective-permute-start(bf16[4,256,256]{2,1,0:T(8,128)(2,1)S(1)} %shard_map.49.mine_ref), channel_id=1, source_target_pairs={{0,16},{16,0},{32,48},{48,32},{64,80},{80,64},{96,112},{112,96},{1... | collective-permute-start | bytes 1572872 | tf_op jit(solution)/shard_map/ppermute | solution.py:186
  71.1 0.0 collective-permute-done.4.others_ref
  71.1 4.4 %shard_map.51.start_ref = f32[4,512,256]{2,1,0:T(8,128)S(1)} custom-call(bf16[2,4,512,256]{3,2,1,0:T(8,128)(2,1)S(1)} %get-tuple-element.7.ints_ref, bf16[3,4,256,256]{3,2,1,0:T(8,128)(2,1)S(1)} %shard_map.50.near_ref, bf16[3,4,256,256]{3,2,1,0:T(8,128)(2,1)S(1)} %collective-permute-done.4.others_ref), custom_call_target="tpu_custom_call" | custom-call | flops 1610612736 | bytes 262144 | tf_op jit(solution)/shard_map/pallas_call | solution.py:145
  75.5 0.0 collective-permute-done.2.other_ref
  75.5 3.1 %shard_map.52 = f32[512,1024]{1,0:T(8,128)} custom-call(bf16[2,4,512,256]{3,2,1,0:T(8,128)(2,1)S(1)} %get-tuple-element.7.ints_ref, bf16[4,256,256]{2,1,0:T(8,128)(2,1)S(1)} %shard_map.49.mine_ref, bf16[4,256,256]{2,1,0:T(8,128)(2,1)S(1)} %collective-permute-done.2.other_ref, f32[4,512,256]{2,1,0:T(8,128)S(1)} %get-tuple-element.8.later_ref.scale_ref, ...), custom_call_target="tpu_custom_call" | custom-call | flops 536870912 | bytes 262144 | tf_op jit(solution)/shard_map/pallas_call | solution.py:145
  (3 shorter events, 0.1 us)
Async XLA Ops:
  0.0 46.1 %copy-start.1 = (f32[1024]{0:T(1024)S(1)}, f32[1024]{0:T(1024)}, u32[]{:S(2)}) copy-start(f32[1024]{0:T(1024)} %param.7) | copy-start | bytes 12292
  0.0 46.1 %copy-start.2 = (f32[512]{0:T(512)S(1)}, f32[512]{0:T(512)}, u32[]{:S(2)}) copy-start(f32[512]{0:T(512)} %virt_ref.1) | copy-start | bytes 6148
  0.0 46.1 %copy-start = (bf16[16,32,2048]{2,1,0:T(8,128)(2,1)S(1)}, bf16[16,32,2048]{2,1,0:T(8,128)(2,1)}, u32[]{:S(2)}) copy-start(bf16[16,32,2048]{2,1,0:T(8,128)(2,1)} %param.5) | copy-start | bytes 6291460
  39.6 11.4 %collective-permute-start = (bf16[4,256,256]{2,1,0:T(8,128)(2,1)S(1)}, bf16[4,256,256]{2,1,0:T(8,128)(2,1)S(1)}, u32[]{:S(2)}, u32[]{:S(2)}) collective-permute-start(bf16[4,256,256]{2,1,0:T(8,128)(2,1)S(1)} %all_to_all.11.later_ref.refs_0_), channel_id=1, source_target_pairs={{0,4},{16,144},{32,36},{48,176},{64,68},{80,208},{96,100},{112,240... | collective-permute-start | bytes 1572872 | tf_op jit(solution)/shard_map/ppermute | solution.py:172
  42.7 10.3 %collective-permute-start.3 = (bf16[4,256,256]{2,1,0:T(8,128)(2,1)S(1)}, bf16[4,256,256]{2,1,0:T(8,128)(2,1)S(1)}, u32[]{:S(2)}, u32[]{:S(2)}) collective-permute-start(bf16[4,256,256]{2,1,0:T(8,128)(2,1)S(1)} %all_to_all.11.later_ref.refs_0_), channel_id=1, source_target_pairs={{0,12},{16,400},{32,44},{48,432},{64,76},{80,464},{96,108},{112,49... | collective-permute-start | bytes 1572872 | tf_op jit(solution)/shard_map/ppermute | solution.py:173
  51.0 11.1 %collective-permute-start.1 = (bf16[4,256,256]{2,1,0:T(8,128)(2,1)S(1)}, bf16[4,256,256]{2,1,0:T(8,128)(2,1)S(1)}, u32[]{:S(2)}, u32[]{:S(2)}) collective-permute-start(bf16[4,256,256]{2,1,0:T(8,128)(2,1)S(1)} %shard_map.48), channel_id=1, source_target_pairs={{0,4},{16,144},{32,36},{48,176},{64,68},{80,208},{96,100},{112,240... | collective-permute-start | bytes 1572872 | tf_op jit(solution)/shard_map/ppermute | solution.py:182
  53.1 18.0 %collective-permute-start.4 = (bf16[3,4,256,256]{3,2,1,0:T(8,128)(2,1)S(1)}, bf16[3,4,256,256]{3,2,1,0:T(8,128)(2,1)S(1)}, u32[]{:S(2)}, u32[]{:S(2)}) collective-permute-start(bf16[3,4,256,256]{3,2,1,0:T(8,128)(2,1)S(1)} %shard_map.50.near_ref), channel_id=1, source_target_pairs={{0,16},{16,0},{32,48},{48,32},{64,80},{80,64},{96,112},{112,96},{1... | collective-permute-start | bytes 4718600 | tf_op jit(solution)/shard_map/ppermute | solution.py:184
  62.2 13.3 %collective-permute-start.2 = (bf16[4,256,256]{2,1,0:T(8,128)(2,1)S(1)}, bf16[4,256,256]{2,1,0:T(8,128)(2,1)S(1)}, u32[]{:S(2)}, u32[]{:S(2)}) collective-permute-start(bf16[4,256,256]{2,1,0:T(8,128)(2,1)S(1)} %shard_map.49.mine_ref), channel_id=1, source_target_pairs={{0,16},{16,0},{32,48},{48,32},{64,80},{80,64},{96,112},{112,96},{1... | collective-permute-start | bytes 1572872 | tf_op jit(solution)/shard_map/ppermute | solution.py:186

commit v3 on v2

v3 whole, which is shorter than its diff:
```python
import jax
import jax.numpy as jnp
from jax import lax
from jax.experimental import pallas as pl
from jax.experimental.pallas import tpu as pltpu
from jax.sharding import PartitionSpec as P

AXES = ("aa", "ba")
SIDE = 4
DEPTH = 16
FIRSTS, SECONDS = 16, 32
TILE = 256


def flat(x, y, z, core):
    z_hi, z_lo = divmod(z % DEPTH, SIDE)
    return (((x % SIDE) * SIDE + z_lo) * 2 + core) * DEPTH + (y % SIDE) * SIDE + z_hi


def everywhere():
    return [
        (x, y, z, core)
        for x in range(SIDE) for y in range(SIDE) for z in range(DEPTH) for core in range(2)
    ]


def z_groups():
    return [
        [flat(x, y, z, core) for z in range(DEPTH)]
        for x in range(SIDE) for y in range(SIDE) for core in range(2)
    ]


def plane_groups(x_core):
    return [
        [flat(i, u, z, core) if core == x_core else flat(u, i, z, core) for i in range(SIDE)]
        for u in range(SIDE) for z in range(DEPTH) for core in range(2)
    ]


def core_swap():
    return [(flat(x, y, z, core), flat(x, y, z, 1 - core)) for x, y, z, core in everywhere()]


def line_kernel(in_ref, out_ref):
    low = lax.broadcasted_iota(jnp.int32, (32, 128), 1) < 64
    for z_hi in range(SIDE):
        for half in range(2):
            first = in_ref[z_hi * SIDE + 2 * half]
            second = in_ref[z_hi * SIDE + 2 * half + 1]
            upper = jnp.where(low, first, pltpu.roll(second, 64, 1))
            lower = jnp.where(low, pltpu.roll(first, 64, 1), second)
            row, column = z_hi * 64, half * 128
            for copy in range(SIDE):
                out_ref[copy, row : row + 32, column : column + 128] = upper
                out_ref[copy, row + 32 : row + 64, column : column + 128] = lower


def repeat_kernel(in_ref, out_ref):
    for copy in range(SIDE):
        out_ref[copy] = in_ref[...]


def multiply(ints, amps):
    return lax.dot_general(ints, amps, (((1,), (1,)), ((), ())), preferred_element_type=jnp.float32)


def begin_kernel(virt_ref, raw_ref, pair_ref, mine_ref, ints_ref, scale_ref, total_ref):
    rows = raw_ref.shape[0]
    low = lax.broadcasted_iota(jnp.int32, (rows, 128), 1) < 64
    for x in range(SIDE):
        for half in range(2):
            column = x * 512 + half * 256
            first = raw_ref[:, column : column + 128]
            second = raw_ref[:, column + 128 : column + 256]
            to = slice(x * TILE + half * 128, x * TILE + half * 128 + 128)
            ints_ref[0, :, to] = jnp.where(low, first, pltpu.roll(second, 64, 1))
            ints_ref[1, :, to] = jnp.where(low, pltpu.roll(first, 64, 1), second)
    first_at, second_at = lax.axis_index("aa") * FIRSTS, lax.axis_index("ba") * SECONDS
    row = lax.broadcasted_iota(jnp.int32, (SECONDS, TILE), 0)
    seconds = jnp.zeros((SECONDS, TILE), jnp.float32)
    for b in range(SECONDS):
        seconds = jnp.where(row == b, virt_ref[second_at + b], seconds)
    for y in range(SIDE):
        to = slice(y * TILE, y * TILE + TILE)
        pair = pair_ref[:, to]
        for a in range(FIRSTS):
            denominator = virt_ref[first_at + a] + seconds + pair
            scale_ref[a * SECONDS : (a + 1) * SECONDS, to] = 1.0 / denominator
    core = lax.rem(lax.axis_index("aa"), 2)

    def put(y, product):
        total_ref[:, y * TILE : y * TILE + TILE] = product

    add_half(core, ints_ref, mine_ref, put)


def add_half(core, ints_ref, amps_ref, put):
    for of_core in range(2):
        @pl.when(core == of_core)
        def _():
            for y in range(SIDE):
                tiles = [amps_ref[y, x] if of_core == 0 else amps_ref[x, y] for x in range(SIDE)]
                put(y, multiply(ints_ref[of_core], jnp.concatenate(tiles, axis=1)))


def end_kernel(ints_ref, other_ref, scale_ref, start_ref, out_ref):
    core = 1 - lax.rem(lax.axis_index("aa"), 2)

    def put(y, product):
        to = slice(y * TILE, y * TILE + TILE)
        out_ref[:, to] = (start_ref[:, to] + product) * scale_ref[:, to]

    add_half(core, ints_ref, other_ref, put)


SMEM = pl.BlockSpec(memory_space=pltpu.SMEM)
VMEM = pl.BlockSpec(memory_space=pltpu.VMEM)


def call(kernel, ins, outs, specs=None, scratch=(), tiles=0, megabytes=16):
    return pl.pallas_call(
        kernel,
        out_shape=outs,
        in_specs=specs or [VMEM] * len(ins),
        out_specs=jax.tree.map(lambda _: VMEM, outs),
        scratch_shapes=list(scratch),
        compiler_params=pltpu.CompilerParams(vmem_limit_bytes=megabytes * 2**20),
        cost_estimate=pl.CostEstimate(
            flops=tiles * 2 * 512 * TILE * TILE, bytes_accessed=2**18, transcendentals=0
        ),
    )(*ins)


def bf16(*shape):
    return jax.ShapeDtypeStruct(shape, jnp.bfloat16)


def on_device(amplitudes, integrals, virt_energy, pair_energy):
    first_count, second_count, cd_count = integrals.shape
    rows, pairs = first_count * second_count, pair_energy.shape[0]

    packed = jnp.concatenate([amplitudes[:32], amplitudes[32:]], axis=1)
    sent = jnp.broadcast_to(packed[None], (DEPTH, 32, 128))
    lines = lax.all_to_all(sent, AXES, 0, 0, axis_index_groups=z_groups(), tiled=True)
    sent = call(line_kernel, (lines,), bf16(SIDE, TILE, TILE), megabytes=4)
    mine = lax.all_to_all(sent, AXES, 0, 0, axis_index_groups=plane_groups(0), tiled=True)

    mine = call(repeat_kernel, (mine,), bf16(SIDE, SIDE, TILE, TILE), megabytes=6)
    mine = lax.all_to_all(mine, AXES, 0, 0, axis_index_groups=plane_groups(1), tiled=True)
    other = lax.ppermute(mine, AXES, core_swap())
    totals = jax.ShapeDtypeStruct((rows, pairs), jnp.float32)
    ints, scale, total = call(
        begin_kernel,
        (virt_energy, integrals.reshape(rows, cd_count), pair_energy.reshape(1, -1), mine),
        (bf16(2, rows, SIDE * TILE), totals, totals),
        specs=[SMEM, VMEM, VMEM, VMEM], tiles=16,
    )
    update = call(end_kernel, (ints, other, scale, total), totals, tiles=16)
    return update.reshape(first_count, second_count, pairs)


def solution(mesh):
    placed = (P("ba", "aa"), P("aa", "ba", None), P(), P())
    return jax.shard_map(
        on_device, mesh=mesh, in_specs=placed, out_specs=P("aa", "ba", None), check_vma=False
    )
```

time: 79 us -> 74 us (0.937)
  blocking collectives: 38.5 us -> 58.1 us
  starting transfers between devices: 25.3 us -> 8.12 us
  waiting for transfers between devices: 4.45 us -> 0.84 us
  Pallas kernels: 9.36 us -> 5.79 us
    all_to_all x1 -> x2, blocking collectives: 10.9 us -> 30.5 us  [the longest x1 19.6 us: on_device(): lax.all_to_all(mine, AXES, 0, 0, axis_index_groups=plane_groups(1), tiled...]
    ppermute x5 -> x1, starting transfers between devices: 25.3 us -> 8.12 us  [on_device(): other = lax.ppermute(mine, AXES, core_swap())]
    ppermute x5 -> x1, waiting for transfers between devices: 4.45 us -> 0.84 us  [on_device(): other = lax.ppermute(mine, AXES, core_swap())]
    pallas_call x7 -> x4, Pallas kernels: 9.36 us -> 5.79 us  [call(): pl.pallas_call(kernel, out_shape=outs, in_specs=specs or [VMEM] * len(ins...]
  transfers between devices with their start and end apart: 5 -> 1, of which waited for: 2 -> 1; matrix products, arithmetic and copies ran while one was open for 0% -> 0% of each run, Pallas kernels for 8% -> 4%
where the time goes in v3:
time: 74 us; the launch traced here: 73.7 us
  blocking collectives  58.1 us (79%)
  starting transfers between devices  8.12 us (11%)
  Pallas kernels  5.79 us (8%)
  waiting for transfers between devices  0.84 us (1%)
  local copies, waits for them, and re-layouts  0.76 us (1%)
    all_to_all x1, blocking collectives, on_device(): lax.all_to_all(sent, AXES, 0, 0, axis_index_groups=z_groups(), tiled=True)  27.5 us
    all_to_all x1, blocking collectives, on_device(): lax.all_to_all(mine, AXES, 0, 0, axis_index_groups=plane_groups(1), tiled...  19.6 us
    all_to_all x1, blocking collectives, on_device(): lax.all_to_all(sent, AXES, 0, 0, axis_index_groups=plane_groups(0), tiled...  10.9 us
    ppermute x1, starting transfers between devices, on_device(): other = lax.ppermute(mine, AXES, core_swap())  8.12 us
    pallas_call x4, Pallas kernels, call(): pl.pallas_call(kernel, out_shape=outs, in_specs=specs or [VMEM] * len(ins...  5.79 us
  transfers between devices with their start and end apart: 1, of which 1 were waited for; matrix products, arithmetic and copies ran while one was open for 0% of the time, Pallas kernels for 4%

profile of v3, /device:TPU:1, one launch (start us, length us, event | category | flops | bytes accessed | tf_op | source)
XLA Modules:
  0.0 73.7 jit_solution(8537663563729660673)
XLA Ops:
  0.0 0.7 fusion
  0.7 0.1 pad_maximum_fusion
  0.8 27.5 %all_to_all.15.in_ref = bf16[16,32,128]{2,1,0:T(8,128)(2,1)S(1)} all-to-all(bf16[16,32,128]{2,1,0:T(8,128)(2,1)S(1)} %broadcast_in_dim.2), channel_id=1, replica_groups={{0,32,64,96,1,33,65,97,2,34,66,98,3,35,67,99},{16,48,80,112,17,49,81,11..., dimensions={0} | all-to-all | bytes 262144 | tf_op jit(solution)/shard_map/all_to_all | solution.py:145
  28.4 0.1 shard_map.46
  28.5 10.9 %all_to_all.16.in_ref = bf16[4,256,256]{2,1,0:T(8,128)(2,1)S(1)} all-to-all(bf16[4,256,256]{2,1,0:T(8,128)(2,1)S(1)} %shard_map.46), channel_id=1, replica_groups={{0,128,256,384},{16,20,24,28},{32,160,288,416},{48,52,56,60},{64,192,32..., dimensions={0} | all-to-all | bytes 1048576 | tf_op jit(solution)/shard_map/all_to_all | solution.py:147
  39.4 0.1 shard_map.47
  39.6 0.0 copy-start
  39.6 0.0 copy-start.1
  39.6 0.0 copy-start.2
  39.6 19.6 %all_to_all.17.mine_ref = bf16[4,4,256,256]{3,2,1,0:T(8,128)(2,1)S(1)} all-to-all(bf16[4,4,256,256]{3,2,1,0:T(8,128)(2,1)S(1)} %shard_map.47), channel_id=1, replica_groups={{0,4,8,12},{16,144,272,400},{32,36,40,44},{48,176,304,432},{64,68,72,76..., dimensions={0} | all-to-all | bytes 4194304 | tf_op jit(solution)/shard_map/all_to_all | solution.py:150
  59.2 8.1 %collective-permute-start = (bf16[4,4,256,256]{3,2,1,0:T(8,128)(2,1)S(1)}, bf16[4,4,256,256]{3,2,1,0:T(8,128)(2,1)S(1)}, u32[]{:S(2)}, u32[]{:S(2)}) collective-permute-start(bf16[4,4,256,256]{3,2,1,0:T(8,128)(2,1)S(1)} %all_to_all.17.mine_ref), channel_id=1, source_target_pairs={{0,16},{16,0},{32,48},{48,32},{64,80},{80,64},{96,112},{112,96},{1... | collective-permute-start | bytes 6291464 | tf_op jit(solution)/shard_map/ppermute | solution.py:151
  67.3 0.0 copy-done
  67.3 0.0 copy-done.1
  67.3 0.0 copy-done.2
  67.4 2.9 %shard_map.48 = (bf16[2,512,1024]{2,1,0:T(8,128)(2,1)S(1)}, f32[512,1024]{1,0:T(8,128)S(1)}, f32[512,1024]{1,0:T(8,128)S(1)}) custom-call(f32[512]{0:T(512)S(1)} %copy-done.2, bf16[512,2048]{1,0:T(8,128)(2,1)S(1)} %bitcast.3, f32[1,1024]{1,0:T(1,128)S(1)} %bitcast.4, bf16[4,4,256,256]{3,2,1,0:T(8,128)(2,1)S(1)} %all_to_all.17.mine_ref), custom_call_target="tpu_custom_call" | custom-call | flops 1073741824 | bytes 262144 | tf_op jit(solution)/shard_map/pallas_call | solution.py:122
  70.2 0.8 %collective-permute-done.other_ref = bf16[4,4,256,256]{3,2,1,0:T(8,128)(2,1)S(1)} collective-permute-done((bf16[4,4,256,256]{3,2,1,0:T(8,128)(2,1)S(1)}, bf16[4,4,256,256]{3,2,1,0:T(8,128)(2,1)S(1)}, u32[]{:S(2)}, u32[]{:S(2)}) %collective-permute-start) | collective-permute-done | bytes 2097184 | tf_op jit(solution)/shard_map/ppermute | solution.py:151
  71.1 2.6 %shard_map.49 = f32[512,1024]{1,0:T(8,128)} custom-call(bf16[2,512,1024]{2,1,0:T(8,128)(2,1)S(1)} %get-tuple-element.8.ints_ref, bf16[4,4,256,256]{3,2,1,0:T(8,128)(2,1)S(1)} %collective-permute-done.other_ref, f32[512,1024]{1,0:T(8,128)S(1)} %get-tuple-element.9.scale_ref, f32[512,1024]{1,0:T(8,128)S(1)} %get-tuple-element.10.start_ref), custom_call_target="tpu_custom_call" | custom-call | flops 1073741824 | bytes 262144 | tf_op jit(solution)/shard_map/pallas_call | solution.py:122
  (1 shorter events, 0.0 us)
Async XLA Ops:
  39.6 27.8 %copy-start = (bf16[16,32,2048]{2,1,0:T(8,128)(2,1)S(1)}, bf16[16,32,2048]{2,1,0:T(8,128)(2,1)}, u32[]{:S(2)}) copy-start(bf16[16,32,2048]{2,1,0:T(8,128)(2,1)} %param.5) | copy-start | bytes 6291460
  39.6 27.8 %copy-start.1 = (f32[1024]{0:T(1024)S(1)}, f32[1024]{0:T(1024)}, u32[]{:S(2)}) copy-start(f32[1024]{0:T(1024)} %param.7) | copy-start | bytes 12292
  39.6 27.8 %copy-start.2 = (f32[512]{0:T(512)S(1)}, f32[512]{0:T(512)}, u32[]{:S(2)}) copy-start(f32[512]{0:T(512)} %virt_ref.1) | copy-start | bytes 6148
  59.2 11.9 %collective-permute-start = (bf16[4,4,256,256]{3,2,1,0:T(8,128)(2,1)S(1)}, bf16[4,4,256,256]{3,2,1,0:T(8,128)(2,1)S(1)}, u32[]{:S(2)}, u32[]{:S(2)}) collective-permute-start(bf16[4,4,256,256]{3,2,1,0:T(8,128)(2,1)S(1)} %all_to_all.17.mine_ref), channel_id=1, source_target_pairs={{0,16},{16,0},{32,48},{48,32},{64,80},{80,64},{96,112},{112,96},{1... | collective-permute-start | bytes 6291464 | tf_op jit(solution)/shard_map/ppermute | solution.py:151

commit v4 on v3

--- a/solution.py
+++ b/solution.py
@@ -38,6 +38,13 @@
     ]
 
 
+def xy_groups():
+    return [
+        [flat(x, y, z, core) for y in range(SIDE) for x in range(SIDE)]
+        for z in range(DEPTH) for core in range(2)
+    ]
+
+
 def core_swap():
     return [(flat(x, y, z, core), flat(x, y, z, 1 - core)) for x, y, z, core in everywhere()]
 
@@ -51,7 +58,7 @@
             upper = jnp.where(low, first, pltpu.roll(second, 64, 1))
             lower = jnp.where(low, pltpu.roll(first, 64, 1), second)
             row, column = z_hi * 64, half * 128
-            for copy in range(SIDE):
+            for copy in range(SIDE * SIDE):
                 out_ref[copy, row : row + 32, column : column + 128] = upper
                 out_ref[copy, row + 32 : row + 64, column : column + 128] = lower
 
@@ -100,30 +107,37 @@
         @pl.when(core == of_core)
         def _():
             for y in range(SIDE):
-                tiles = [amps_ref[y, x] if of_core == 0 else amps_ref[x, y] for x in range(SIDE)]
+                tiles = [amps_ref[y, x] for x in range(SIDE)]
                 put(y, multiply(ints_ref[of_core], jnp.concatenate(tiles, axis=1)))
 
 
-def end_kernel(ints_ref, other_ref, scale_ref, start_ref, out_ref):
+def end_kernel(ints_ref, other_ref, scale_ref, start_ref, out_ref, held_ref, sems):
     core = 1 - lax.rem(lax.axis_index("aa"), 2)
+
+    def copy(y):
+        to = slice(y * TILE, y * TILE + TILE)
+        return pltpu.make_async_copy(held_ref.at[y], out_ref.at[:, to], sems.at[y])
 
     def put(y, product):
         to = slice(y * TILE, y * TILE + TILE)
-        out_ref[:, to] = (start_ref[:, to] + product) * scale_ref[:, to]
+        held_ref[y] = (start_ref[:, to] + product) * scale_ref[:, to]
+        copy(y).start()
 
     add_half(core, ints_ref, other_ref, put)
+    for y in range(SIDE):
+        copy(y).wait()
 
 
 SMEM = pl.BlockSpec(memory_space=pltpu.SMEM)
 VMEM = pl.BlockSpec(memory_space=pltpu.VMEM)
 
 
-def call(kernel, ins, outs, specs=None, scratch=(), tiles=0, megabytes=16):
+def call(kernel, ins, outs, specs=None, scratch=(), tiles=0, megabytes=16, out_space=pltpu.VMEM):
     return pl.pallas_call(
         kernel,
         out_shape=outs,
         in_specs=specs or [VMEM] * len(ins),
-        out_specs=jax.tree.map(lambda _: VMEM, outs),
+        out_specs=jax.tree.map(lambda _: pl.BlockSpec(memory_space=out_space), outs),
         scratch_shapes=list(scratch),
         compiler_params=pltpu.CompilerParams(vmem_limit_bytes=megabytes * 2**20),
         cost_estimate=pl.CostEstimate(
@@ -143,11 +157,9 @@
     packed = jnp.concatenate([amplitudes[:32], amplitudes[32:]], axis=1)
     sent = jnp.broadcast_to(packed[None], (DEPTH, 32, 128))
     lines = lax.all_to_all(sent, AXES, 0, 0, axis_index_groups=z_groups(), tiled=True)
-    sent = call(line_kernel, (lines,), bf16(SIDE, TILE, TILE), megabytes=4)
-    mine = lax.all_to_all(sent, AXES, 0, 0, axis_index_groups=plane_groups(0), tiled=True)
-
-    mine = call(repeat_kernel, (mine,), bf16(SIDE, SIDE, TILE, TILE), megabytes=6)
-    mine = lax.all_to_all(mine, AXES, 0, 0, axis_index_groups=plane_groups(1), tiled=True)
+    sent = call(line_kernel, (lines,), bf16(SIDE * SIDE, TILE, TILE), megabytes=4)
+    mine = lax.all_to_all(sent, AXES, 0, 0, axis_index_groups=xy_groups(), tiled=True)
+    mine = mine.reshape(SIDE, SIDE, TILE, TILE)
     other = lax.ppermute(mine, AXES, core_swap())
     totals = jax.ShapeDtypeStruct((rows, pairs), jnp.float32)
     ints, scale, total = call(
@@ -156,7 +168,10 @@
         (bf16(2, rows, SIDE * TILE), totals, totals),
         specs=[SMEM, VMEM, VMEM, VMEM], tiles=16,
     )
-    update = call(end_kernel, (ints, other, scale, total), totals, tiles=16)
+    update = call(
+        end_kernel, (ints, other, scale, total), totals, tiles=16, out_space=pl.ANY,
+        scratch=[pltpu.VMEM((SIDE, rows, TILE), jnp.float32), pltpu.SemaphoreType.DMA((SIDE,))],
+    )
     return update.reshape(first_count, second_count, pairs)
 
 

time: 74 us -> 73.2 us (0.989)
  starting transfers between devices: 8.12 us -> 6.71 us
    ppermute x1, starting transfers between devices: 8.12 us -> 6.71 us  [on_device(): other = lax.ppermute(mine, AXES, core_swap())]
    all_to_all x2 -> x1, blocking collectives: 30.5 us -> 31.3 us  [on_device(): lax.all_to_all(sent, AXES, 0, 0, axis_index_groups=xy_groups(), tiled=True)]
    pallas_call x4 -> x3, Pallas kernels: 5.79 us -> 5.65 us  [call(): pl.pallas_call(kernel, out_shape=outs, in_specs=specs or [VMEM] * len(ins...]
where the time goes in v4:
time: 73.2 us; the launch traced here: 73 us
  blocking collectives  58.8 us (80%)
  starting transfers between devices  6.71 us (9%)
  Pallas kernels  5.65 us (8%)
  waiting for transfers between devices  0.84 us (1%)
  local copies, waits for them, and re-layouts  0.76 us (1%)
    all_to_all x1, blocking collectives, on_device(): lax.all_to_all(sent, AXES, 0, 0, axis_index_groups=xy_groups(), tiled=True)  31.3 us
    all_to_all x1, blocking collectives, on_device(): lax.all_to_all(sent, AXES, 0, 0, axis_index_groups=z_groups(), tiled=True)  27.5 us
    ppermute x1, starting transfers between devices, on_device(): other = lax.ppermute(mine, AXES, core_swap())  6.71 us
    pallas_call x3, Pallas kernels, call(): pl.pallas_call(kernel, out_shape=outs, in_specs=specs or [VMEM] * len(ins...  5.65 us
  transfers between devices with their start and end apart: 1, of which 1 were waited for; matrix products, arithmetic and copies ran while one was open for 0% of the time, Pallas kernels for 4%

profile of v4, /device:TPU:1, one launch (start us, length us, event | category | flops | bytes accessed | tf_op | source)
XLA Modules:
  0.0 73.0 jit_solution(16015822808886109106)
XLA Ops:
  0.0 0.7 fusion
  0.7 0.1 pad_maximum_fusion
  0.8 27.5 %all_to_all.10.in_ref = bf16[16,32,128]{2,1,0:T(8,128)(2,1)S(1)} all-to-all(bf16[16,32,128]{2,1,0:T(8,128)(2,1)S(1)} %broadcast_in_dim.2), channel_id=1, replica_groups={{0,32,64,96,1,33,65,97,2,34,66,98,3,35,67,99},{16,48,80,112,17,49,81,11..., dimensions={0} | all-to-all | bytes 262144 | tf_op jit(solution)/shard_map/all_to_all | solution.py:159
  28.4 0.3 shard_map.46
  28.7 0.0 copy-start
  28.7 0.0 copy-start.1
  28.7 0.0 copy-start.2
  28.7 31.3 %all_to_all.11 = bf16[16,256,256]{2,1,0:T(8,128)(2,1)S(1)} all-to-all(bf16[16,256,256]{2,1,0:T(8,128)(2,1)S(1)} %shard_map.46), channel_id=1, replica_groups={{0,128,256,384,4,132,260,388,8,136,264,392,12,140,268,396},{16,144,272,..., dimensions={0} | all-to-all | bytes 4194304 | tf_op jit(solution)/shard_map/all_to_all | solution.py:161
  60.0 6.7 %collective-permute-start = (bf16[4,4,256,256]{3,2,1,0:T(8,128)(2,1)S(1)}, bf16[4,4,256,256]{3,2,1,0:T(8,128)(2,1)S(1)}, u32[]{:S(2)}, u32[]{:S(2)}) collective-permute-start(bf16[4,4,256,256]{3,2,1,0:T(8,128)(2,1)S(1)} %bitcast.4), channel_id=1, source_target_pairs={{0,16},{16,0},{32,48},{48,32},{64,80},{80,64},{96,112},{112,96},{1... | collective-permute-start | bytes 6291464 | tf_op jit(solution)/shard_map/ppermute | solution.py:163
  66.8 0.0 copy-done
  66.8 0.0 copy-done.1
  66.8 0.0 copy-done.2
  66.8 2.9 %shard_map.47 = (bf16[2,512,1024]{2,1,0:T(8,128)(2,1)S(1)}, f32[512,1024]{1,0:T(8,128)S(1)}, f32[512,1024]{1,0:T(8,128)S(1)}) custom-call(f32[512]{0:T(512)S(1)} %copy-done.2, bf16[512,2048]{1,0:T(8,128)(2,1)S(1)} %bitcast.6, f32[1,1024]{1,0:T(1,128)S(1)} %bitcast.7, bf16[4,4,256,256]{3,2,1,0:T(8,128)(2,1)S(1)} %bitcast.5), custom_call_target="tpu_custom_call" | custom-call | flops 1073741824 | bytes 262144 | tf_op jit(solution)/shard_map/pallas_call | solution.py:136
  69.7 0.8 %collective-permute-done.other_ref = bf16[4,4,256,256]{3,2,1,0:T(8,128)(2,1)S(1)} collective-permute-done((bf16[4,4,256,256]{3,2,1,0:T(8,128)(2,1)S(1)}, bf16[4,4,256,256]{3,2,1,0:T(8,128)(2,1)S(1)}, u32[]{:S(2)}, u32[]{:S(2)}) %collective-permute-start) | collective-permute-done | bytes 2097184 | tf_op jit(solution)/shard_map/ppermute | solution.py:163
  70.5 2.4 %shard_map.48 = f32[512,1024]{1,0:T(8,128)} custom-call(bf16[2,512,1024]{2,1,0:T(8,128)(2,1)S(1)} %get-tuple-element.8.ints_ref, bf16[4,4,256,256]{3,2,1,0:T(8,128)(2,1)S(1)} %collective-permute-done.other_ref, f32[512,1024]{1,0:T(8,128)S(1)} %get-tuple-element.9.scale_ref, f32[512,1024]{1,0:T(8,128)S(1)} %get-tuple-element.10.start_ref), custom_call_target="tpu_custom_call" | custom-call | flops 1073741824 | bytes 262144 | tf_op jit(solution)/shard_map/pallas_call | solution.py:136
  (1 shorter events, 0.0 us)
Async XLA Ops:
  28.7 38.1 %copy-start = (bf16[16,32,2048]{2,1,0:T(8,128)(2,1)S(1)}, bf16[16,32,2048]{2,1,0:T(8,128)(2,1)}, u32[]{:S(2)}) copy-start(bf16[16,32,2048]{2,1,0:T(8,128)(2,1)} %param.5) | copy-start | bytes 6291460
  28.7 38.1 %copy-start.1 = (f32[1024]{0:T(1024)S(1)}, f32[1024]{0:T(1024)}, u32[]{:S(2)}) copy-start(f32[1024]{0:T(1024)} %param.7) | copy-start | bytes 12292
  28.7 38.1 %copy-start.2 = (f32[512]{0:T(512)S(1)}, f32[512]{0:T(512)}, u32[]{:S(2)}) copy-start(f32[512]{0:T(512)} %virt_ref.1) | copy-start | bytes 6148
  60.0 10.5 %collective-permute-start = (bf16[4,4,256,256]{3,2,1,0:T(8,128)(2,1)S(1)}, bf16[4,4,256,256]{3,2,1,0:T(8,128)(2,1)S(1)}, u32[]{:S(2)}, u32[]{:S(2)}) collective-permute-start(bf16[4,4,256,256]{3,2,1,0:T(8,128)(2,1)S(1)} %bitcast.4), channel_id=1, source_target_pairs={{0,16},{16,0},{32,48},{48,32},{64,80},{80,64},{96,112},{112,96},{1... | collective-permute-start | bytes 6291464 | tf_op jit(solution)/shard_map/ppermute | solution.py:163

commit v5 on v4

--- a/solution.py
+++ b/solution.py
@@ -8,6 +8,8 @@
 AXES = ("aa", "ba")
 SIDE = 4
 DEPTH = 16
+PLANE = [2, 3, 0, 1]
+ORDER = [10, 11, 12, 13, 14, 15, 0, 1, 2, 3, 4, 5, 6, 7, 8, 9]
 FIRSTS, SECONDS = 16, 32
 TILE = 256
 
@@ -26,22 +28,15 @@
 
 def z_groups():
     return [
-        [flat(x, y, z, core) for z in range(DEPTH)]
+        [flat(x, y, z, core) for z in ORDER]
         for x in range(SIDE) for y in range(SIDE) for core in range(2)
     ]
 
 
 def plane_groups(x_core):
     return [
-        [flat(i, u, z, core) if core == x_core else flat(u, i, z, core) for i in range(SIDE)]
+        [flat(i, u, z, core) if core == x_core else flat(u, i, z, core) for i in PLANE]
         for u in range(SIDE) for z in range(DEPTH) for core in range(2)
-    ]
-
-
-def xy_groups():
-    return [
-        [flat(x, y, z, core) for y in range(SIDE) for x in range(SIDE)]
-        for z in range(DEPTH) for core in range(2)
     ]
 
 
@@ -53,12 +48,12 @@
     low = lax.broadcasted_iota(jnp.int32, (32, 128), 1) < 64
     for z_hi in range(SIDE):
         for half in range(2):
-            first = in_ref[z_hi * SIDE + 2 * half]
-            second = in_ref[z_hi * SIDE + 2 * half + 1]
+            first = in_ref[ORDER.index(z_hi * SIDE + 2 * half)]
+            second = in_ref[ORDER.index(z_hi * SIDE + 2 * half + 1)]
             upper = jnp.where(low, first, pltpu.roll(second, 64, 1))
             lower = jnp.where(low, pltpu.roll(first, 64, 1), second)
             row, column = z_hi * 64, half * 128
-            for copy in range(SIDE * SIDE):
+            for copy in range(SIDE):
                 out_ref[copy, row : row + 32, column : column + 128] = upper
                 out_ref[copy, row + 32 : row + 64, column : column + 128] = lower
 
@@ -107,7 +102,7 @@
         @pl.when(core == of_core)
         def _():
             for y in range(SIDE):
-                tiles = [amps_ref[y, x] for x in range(SIDE)]
+                tiles = [amps_ref[PLANE.index(y), PLANE.index(x)] if of_core == 0 else amps_ref[PLANE.index(x), PLANE.index(y)] for x in range(SIDE)]
                 put(y, multiply(ints_ref[of_core], jnp.concatenate(tiles, axis=1)))
 
 
@@ -157,9 +152,11 @@
     packed = jnp.concatenate([amplitudes[:32], amplitudes[32:]], axis=1)
     sent = jnp.broadcast_to(packed[None], (DEPTH, 32, 128))
     lines = lax.all_to_all(sent, AXES, 0, 0, axis_index_groups=z_groups(), tiled=True)
-    sent = call(line_kernel, (lines,), bf16(SIDE * SIDE, TILE, TILE), megabytes=4)
-    mine = lax.all_to_all(sent, AXES, 0, 0, axis_index_groups=xy_groups(), tiled=True)
-    mine = mine.reshape(SIDE, SIDE, TILE, TILE)
+    sent = call(line_kernel, (lines,), bf16(SIDE, TILE, TILE), megabytes=4)
+    mine = lax.all_to_all(sent, AXES, 0, 0, axis_index_groups=plane_groups(0), tiled=True)
+
+    mine = call(repeat_kernel, (mine,), bf16(SIDE, SIDE, TILE, TILE), megabytes=6)
+    mine = lax.all_to_all(mine, AXES, 0, 0, axis_index_groups=plane_groups(1), tiled=True)
     other = lax.ppermute(mine, AXES, core_swap())
     totals = jax.ShapeDtypeStruct((rows, pairs), jnp.float32)
     ints, scale, total = call(

time: 73.2 us -> 65.6 us (0.90)
  blocking collectives: 58.8 us -> 52.8 us
  starting transfers between devices: 6.71 us -> 5.21 us
    all_to_all x1 -> x2, blocking collectives: 31.3 us -> 28 us  [the longest x1 18.2 us: on_device(): lax.all_to_all(mine, AXES, 0, 0, axis_index_groups=plane_groups(1), tiled...]
    all_to_all x1, blocking collectives: 27.5 us -> 24.8 us  [on_device(): lax.all_to_all(sent, AXES, 0, 0, axis_index_groups=z_groups(), tiled=True)]
    ppermute x1, starting transfers between devices: 6.71 us -> 5.21 us  [on_device(): other = lax.ppermute(mine, AXES, core_swap())]
    pallas_call x3 -> x4, Pallas kernels: 5.65 us -> 5.58 us  [call(): pl.pallas_call(kernel, out_shape=outs, in_specs=specs or [VMEM] * len(ins...]
where the time goes in v5:
time: 65.6 us; the launch traced here: 65.3 us
  blocking collectives  52.8 us (80%)
  Pallas kernels  5.58 us (9%)
  starting transfers between devices  5.21 us (8%)
  waiting for transfers between devices  0.84 us (1%)
  local copies, waits for them, and re-layouts  0.76 us (1%)
    all_to_all x1, blocking collectives, on_device(): lax.all_to_all(sent, AXES, 0, 0, axis_index_groups=z_groups(), tiled=True)  24.8 us
    all_to_all x1, blocking collectives, on_device(): lax.all_to_all(mine, AXES, 0, 0, axis_index_groups=plane_groups(1), tiled...  18.2 us
    all_to_all x1, blocking collectives, on_device(): lax.all_to_all(sent, AXES, 0, 0, axis_index_groups=plane_groups(0), tiled...  9.85 us
    pallas_call x4, Pallas kernels, call(): pl.pallas_call(kernel, out_shape=outs, in_specs=specs or [VMEM] * len(ins...  5.58 us
    ppermute x1, starting transfers between devices, on_device(): other = lax.ppermute(mine, AXES, core_swap())  5.21 us
  transfers between devices with their start and end apart: 1, of which 1 were waited for; matrix products, arithmetic and copies ran while one was open for 0% of the time, Pallas kernels for 4%

profile of v5, /device:TPU:1, one launch (start us, length us, event | category | flops | bytes accessed | tf_op | source)
XLA Modules:
  0.0 65.3 jit_solution(12002867057885579520)
XLA Ops:
  0.0 0.7 %fusion = (bf16[32,64]{1,0:T(8,128)(2,1)S(1)}, bf16[32,64]{1,0:T(8,128)(2,1)S(1)}) fusion(bf16[64,64]{1,0:T(8,128)(2,1)} %param.4), kind=kLoop, calls=%fused_computation.1 | loop fusion | bytes 16384 | tf_op jit(solution)/shard_map/slice | solution.py:152
  0.7 0.1 pad_maximum_fusion
  0.8 24.8 %all_to_all.15.in_ref = bf16[16,32,128]{2,1,0:T(8,128)(2,1)S(1)} all-to-all(bf16[16,32,128]{2,1,0:T(8,128)(2,1)S(1)} %broadcast_in_dim.2), channel_id=1, replica_groups={{66,98,3,35,67,99,0,32,64,96,1,33,65,97,2,34},{82,114,19,51,83,115,16,4..., dimensions={0} | all-to-all | bytes 262144 | tf_op jit(solution)/shard_map/all_to_all | solution.py:154
  25.6 0.1 shard_map.46
  25.7 9.9 %all_to_all.16.in_ref = bf16[4,256,256]{2,1,0:T(8,128)(2,1)S(1)} all-to-all(bf16[4,256,256]{2,1,0:T(8,128)(2,1)S(1)} %shard_map.46), channel_id=1, replica_groups={{256,384,0,128},{24,28,16,20},{288,416,32,160},{56,60,48,52},{320,448,6..., dimensions={0} | all-to-all | bytes 1048576 | tf_op jit(solution)/shard_map/all_to_all | solution.py:156
  35.6 0.1 shard_map.47
  35.7 0.0 copy-start
  35.7 0.0 copy-start.1
  35.7 0.0 copy-start.2
  35.7 18.2 %all_to_all.17.mine_ref = bf16[4,4,256,256]{3,2,1,0:T(8,128)(2,1)S(1)} all-to-all(bf16[4,4,256,256]{3,2,1,0:T(8,128)(2,1)S(1)} %shard_map.47), channel_id=1, replica_groups={{8,12,0,4},{272,400,16,144},{40,44,32,36},{304,432,48,176},{72,76,64,68..., dimensions={0} | all-to-all | bytes 4194304 | tf_op jit(solution)/shard_map/all_to_all | solution.py:159
  53.9 5.2 %collective-permute-start = (bf16[4,4,256,256]{3,2,1,0:T(8,128)(2,1)S(1)}, bf16[4,4,256,256]{3,2,1,0:T(8,128)(2,1)S(1)}, u32[]{:S(2)}, u32[]{:S(2)}) collective-permute-start(bf16[4,4,256,256]{3,2,1,0:T(8,128)(2,1)S(1)} %all_to_all.17.mine_ref), channel_id=1, source_target_pairs={{0,16},{16,0},{32,48},{48,32},{64,80},{80,64},{96,112},{112,96},{1... | collective-permute-start | bytes 6291464 | tf_op jit(solution)/shard_map/ppermute | solution.py:160
  59.1 0.0 copy-done
  59.1 0.0 copy-done.1
  59.1 0.0 copy-done.2
  59.1 2.9 %shard_map.48 = (bf16[2,512,1024]{2,1,0:T(8,128)(2,1)S(1)}, f32[512,1024]{1,0:T(8,128)S(1)}, f32[512,1024]{1,0:T(8,128)S(1)}) custom-call(f32[512]{0:T(512)S(1)} %copy-done.2, bf16[512,2048]{1,0:T(8,128)(2,1)S(1)} %bitcast.3, f32[1,1024]{1,0:T(1,128)S(1)} %bitcast.4, bf16[4,4,256,256]{3,2,1,0:T(8,128)(2,1)S(1)} %all_to_all.17.mine_ref), custom_call_target="tpu_custom_call" | custom-call | flops 1073741824 | bytes 262144 | tf_op jit(solution)/shard_map/pallas_call | solution.py:131
  62.0 0.8 %collective-permute-done.other_ref = bf16[4,4,256,256]{3,2,1,0:T(8,128)(2,1)S(1)} collective-permute-done((bf16[4,4,256,256]{3,2,1,0:T(8,128)(2,1)S(1)}, bf16[4,4,256,256]{3,2,1,0:T(8,128)(2,1)S(1)}, u32[]{:S(2)}, u32[]{:S(2)}) %collective-permute-start) | collective-permute-done | bytes 2097184 | tf_op jit(solution)/shard_map/ppermute | solution.py:160
  62.9 2.4 %shard_map.49 = f32[512,1024]{1,0:T(8,128)} custom-call(bf16[2,512,1024]{2,1,0:T(8,128)(2,1)S(1)} %get-tuple-element.8.ints_ref, bf16[4,4,256,256]{3,2,1,0:T(8,128)(2,1)S(1)} %collective-permute-done.other_ref, f32[512,1024]{1,0:T(8,128)S(1)} %get-tuple-element.9.scale_ref, f32[512,1024]{1,0:T(8,128)S(1)} %get-tuple-element.10.start_ref), custom_call_target="tpu_custom_call" | custom-call | flops 1073741824 | bytes 262144 | tf_op jit(solution)/shard_map/pallas_call | solution.py:131
  (1 shorter events, 0.0 us)
Async XLA Ops:
  35.7 23.4 %copy-start = (bf16[16,32,2048]{2,1,0:T(8,128)(2,1)S(1)}, bf16[16,32,2048]{2,1,0:T(8,128)(2,1)}, u32[]{:S(2)}) copy-start(bf16[16,32,2048]{2,1,0:T(8,128)(2,1)} %param.5) | copy-start | bytes 6291460
  35.7 23.4 %copy-start.1 = (f32[1024]{0:T(1024)S(1)}, f32[1024]{0:T(1024)}, u32[]{:S(2)}) copy-start(f32[1024]{0:T(1024)} %param.7) | copy-start | bytes 12292
  35.7 23.4 %copy-start.2 = (f32[512]{0:T(512)S(1)}, f32[512]{0:T(512)}, u32[]{:S(2)}) copy-start(f32[512]{0:T(512)} %virt_ref.1) | copy-start | bytes 6148
  53.9 9.0 %collective-permute-start = (bf16[4,4,256,256]{3,2,1,0:T(8,128)(2,1)S(1)}, bf16[4,4,256,256]{3,2,1,0:T(8,128)(2,1)S(1)}, u32[]{:S(2)}, u32[]{:S(2)}) collective-permute-start(bf16[4,4,256,256]{3,2,1,0:T(8,128)(2,1)S(1)} %all_to_all.17.mine_ref), channel_id=1, source_target_pairs={{0,16},{16,0},{32,48},{48,32},{64,80},{80,64},{96,112},{112,96},{1... | collective-permute-start | bytes 6291464 | tf_op jit(solution)/shard_map/ppermute | solution.py:160

commit v6 on v5

--- a/solution.py
+++ b/solution.py
@@ -9,7 +9,7 @@
 SIDE = 4
 DEPTH = 16
 PLANE = [2, 3, 0, 1]
-ORDER = [10, 11, 12, 13, 14, 15, 0, 1, 2, 3, 4, 5, 6, 7, 8, 9]
+ORDER = [12, 13, 14, 15, 0, 1, 2, 3, 4, 5, 6, 7, 8, 9, 10, 11]
 FIRSTS, SECONDS = 16, 32
 TILE = 256
 

time: 65.6 us -> 66.9 us (1.020)
    all_to_all x1, blocking collectives: 24.8 us -> 25.5 us  [on_device(): lax.all_to_all(sent, AXES, 0, 0, axis_index_groups=z_groups(), tiled=True)]
where the time goes in v6:
time: 66.9 us; the launch traced here: 66.5 us
  blocking collectives  53.4 us (80%)
  starting transfers between devices  5.81 us (9%)
  Pallas kernels  5.58 us (8%)
  waiting for transfers between devices  0.84 us (1%)
  local copies, waits for them, and re-layouts  0.76 us (1%)
    all_to_all x1, blocking collectives, on_device(): lax.all_to_all(sent, AXES, 0, 0, axis_index_groups=z_groups(), tiled=True)  25.5 us
    all_to_all x1, blocking collectives, on_device(): lax.all_to_all(mine, AXES, 0, 0, axis_index_groups=plane_groups(1), tiled...  18 us
    all_to_all x1, blocking collectives, on_device(): lax.all_to_all(sent, AXES, 0, 0, axis_index_groups=plane_groups(0), tiled...  9.85 us
    ppermute x1, starting transfers between devices, on_device(): other = lax.ppermute(mine, AXES, core_swap())  5.81 us
    pallas_call x4, Pallas kernels, call(): pl.pallas_call(kernel, out_shape=outs, in_specs=specs or [VMEM] * len(ins...  5.58 us
  transfers between devices with their start and end apart: 1, of which 1 were waited for; matrix products, arithmetic and copies ran while one was open for 0% of the time, Pallas kernels for 4%

profile of v6, /device:TPU:1, one launch (start us, length us, event | category | flops | bytes accessed | tf_op | source)
XLA Modules:
  0.0 66.5 jit_solution(1593486947539241240)
XLA Ops:
  0.0 0.7 %fusion = (bf16[32,64]{1,0:T(8,128)(2,1)S(1)}, bf16[32,64]{1,0:T(8,128)(2,1)S(1)}) fusion(bf16[64,64]{1,0:T(8,128)(2,1)} %param.4), kind=kLoop, calls=%fused_computation.1 | loop fusion | bytes 16384 | tf_op jit(solution)/shard_map/slice | solution.py:152
  0.7 0.1 pad_maximum_fusion
  0.8 25.5 %all_to_all.15.in_ref = bf16[16,32,128]{2,1,0:T(8,128)(2,1)S(1)} all-to-all(bf16[16,32,128]{2,1,0:T(8,128)(2,1)S(1)} %broadcast_in_dim.2), channel_id=1, replica_groups={{3,35,67,99,0,32,64,96,1,33,65,97,2,34,66,98},{19,51,83,115,16,48,80,11..., dimensions={0} | all-to-all | bytes 262144 | tf_op jit(solution)/shard_map/all_to_all | solution.py:154
  26.3 0.1 shard_map.46
  26.5 9.9 %all_to_all.16.in_ref = bf16[4,256,256]{2,1,0:T(8,128)(2,1)S(1)} all-to-all(bf16[4,256,256]{2,1,0:T(8,128)(2,1)S(1)} %shard_map.46), channel_id=1, replica_groups={{256,384,0,128},{24,28,16,20},{288,416,32,160},{56,60,48,52},{320,448,6..., dimensions={0} | all-to-all | bytes 1048576 | tf_op jit(solution)/shard_map/all_to_all | solution.py:156
  36.3 0.1 shard_map.47
  36.5 0.0 copy-start
  36.5 0.0 copy-start.1
  36.5 0.0 copy-start.2
  36.5 18.0 %all_to_all.17.mine_ref = bf16[4,4,256,256]{3,2,1,0:T(8,128)(2,1)S(1)} all-to-all(bf16[4,4,256,256]{3,2,1,0:T(8,128)(2,1)S(1)} %shard_map.47), channel_id=1, replica_groups={{8,12,0,4},{272,400,16,144},{40,44,32,36},{304,432,48,176},{72,76,64,68..., dimensions={0} | all-to-all | bytes 4194304 | tf_op jit(solution)/shard_map/all_to_all | solution.py:159
  54.5 5.8 %collective-permute-start = (bf16[4,4,256,256]{3,2,1,0:T(8,128)(2,1)S(1)}, bf16[4,4,256,256]{3,2,1,0:T(8,128)(2,1)S(1)}, u32[]{:S(2)}, u32[]{:S(2)}) collective-permute-start(bf16[4,4,256,256]{3,2,1,0:T(8,128)(2,1)S(1)} %all_to_all.17.mine_ref), channel_id=1, source_target_pairs={{0,16},{16,0},{32,48},{48,32},{64,80},{80,64},{96,112},{112,96},{1... | collective-permute-start | bytes 6291464 | tf_op jit(solution)/shard_map/ppermute | solution.py:160
  60.3 0.0 copy-done
  60.4 0.0 copy-done.1
  60.4 0.0 copy-done.2
  60.4 2.9 %shard_map.48 = (bf16[2,512,1024]{2,1,0:T(8,128)(2,1)S(1)}, f32[512,1024]{1,0:T(8,128)S(1)}, f32[512,1024]{1,0:T(8,128)S(1)}) custom-call(f32[512]{0:T(512)S(1)} %copy-done.2, bf16[512,2048]{1,0:T(8,128)(2,1)S(1)} %bitcast.3, f32[1,1024]{1,0:T(1,128)S(1)} %bitcast.4, bf16[4,4,256,256]{3,2,1,0:T(8,128)(2,1)S(1)} %all_to_all.17.mine_ref), custom_call_target="tpu_custom_call" | custom-call | flops 1073741824 | bytes 262144 | tf_op jit(solution)/shard_map/pallas_call | solution.py:131
  63.3 0.8 %collective-permute-done.other_ref = bf16[4,4,256,256]{3,2,1,0:T(8,128)(2,1)S(1)} collective-permute-done((bf16[4,4,256,256]{3,2,1,0:T(8,128)(2,1)S(1)}, bf16[4,4,256,256]{3,2,1,0:T(8,128)(2,1)S(1)}, u32[]{:S(2)}, u32[]{:S(2)}) %collective-permute-start) | collective-permute-done | bytes 2097184 | tf_op jit(solution)/shard_map/ppermute | solution.py:160
  64.1 2.4 %shard_map.49 = f32[512,1024]{1,0:T(8,128)} custom-call(bf16[2,512,1024]{2,1,0:T(8,128)(2,1)S(1)} %get-tuple-element.8.ints_ref, bf16[4,4,256,256]{3,2,1,0:T(8,128)(2,1)S(1)} %collective-permute-done.other_ref, f32[512,1024]{1,0:T(8,128)S(1)} %get-tuple-element.9.scale_ref, f32[512,1024]{1,0:T(8,128)S(1)} %get-tuple-element.10.start_ref), custom_call_target="tpu_custom_call" | custom-call | flops 1073741824 | bytes 262144 | tf_op jit(solution)/shard_map/pallas_call | solution.py:131
  (1 shorter events, 0.0 us)
Async XLA Ops:
  36.5 23.9 %copy-start = (bf16[16,32,2048]{2,1,0:T(8,128)(2,1)S(1)}, bf16[16,32,2048]{2,1,0:T(8,128)(2,1)}, u32[]{:S(2)}) copy-start(bf16[16,32,2048]{2,1,0:T(8,128)(2,1)} %param.5) | copy-start | bytes 6291460
  36.5 23.9 %copy-start.1 = (f32[1024]{0:T(1024)S(1)}, f32[1024]{0:T(1024)}, u32[]{:S(2)}) copy-start(f32[1024]{0:T(1024)} %param.7) | copy-start | bytes 12292
  36.5 23.9 %copy-start.2 = (f32[512]{0:T(512)S(1)}, f32[512]{0:T(512)}, u32[]{:S(2)}) copy-start(f32[512]{0:T(512)} %virt_ref.1) | copy-start | bytes 6148
  54.5 9.6 %collective-permute-start = (bf16[4,4,256,256]{3,2,1,0:T(8,128)(2,1)S(1)}, bf16[4,4,256,256]{3,2,1,0:T(8,128)(2,1)S(1)}, u32[]{:S(2)}, u32[]{:S(2)}) collective-permute-start(bf16[4,4,256,256]{3,2,1,0:T(8,128)(2,1)S(1)} %all_to_all.17.mine_ref), channel_id=1, source_target_pairs={{0,16},{16,0},{32,48},{48,32},{64,80},{80,64},{96,112},{112,96},{1... | collective-permute-start | bytes 6291464 | tf_op jit(solution)/shard_map/ppermute | solution.py:160
